TPU v7x, 256 devices: a whole 4x4x8 slice. The times are simulated.
256 devices in a mesh: seq: 64 (over y_lo, z, x), chan: 4 (over y_hi, core).
Axes of the slice: x: 4, y: 4 (y_hi: 2, y_lo: 2; y = y_hi * 2 + y_lo), z: 8, core: 2. Of those that a mesh axis runs over, the one named last changes fastest.
Arguments:
- features: bfloat16 [16384, 4096], P('seq', 'chan'), may hold values from -6 to 6
- w_in: bfloat16 [4096, 3, 2048], P('seq', None, 'chan'), may hold values from -0.09375 to 0.09375
- filter_real: float32 [16384, 2048], P('seq', 'chan'), may hold values from -6 to 6
- filter_imag: float32 [16384, 2048], P('seq', 'chan'), may hold values from -6 to 6
- skip_gain: float32 [2048], P('chan'), may hold values from -4 to 4
Outputs:
- gated_output: bfloat16 [16384, 2048], P('seq', 'chan')
All inputs are finite; a program needn't handle non-finite values.
Results may differ from a plain program's by a relative error of at most 0.0064.
Values may be sent and summed in bfloat16 or wider, within the bound.
A program may use at most 128 MiB of HBM per device.

v0:
```python
import math
import jax
import jax.numpy as jnp
from jax import lax
from jax.sharding import PartitionSpec as P

TWO_PI = 2.0 * math.pi
HIGHEST = lax.Precision.HIGHEST


def swapped(block, axis, distance):
    count = lax.axis_size(axis)
    route = []
    for low in range(count):
        high = low | 1 << distance
        if high != low and high < count:
            route += [(low, high), (high, low)]
    return lax.ppermute(block, axis, route)


def fold_into(gathered):

    def add_rows(running, panel, offset):
        return jnp.dot(
            gathered, panel.reshape(panel.shape[0], -1), preferred_element_type=jnp.float32
        )

    return add_rows


def twiddle(my_index, level, row_count):
    span = 1 << level
    positions = my_index % span * row_count + jnp.arange(row_count, dtype=jnp.int32)
    angles = -TWO_PI / (2 * span * row_count) * positions.astype(jnp.float32)
    return (jnp.cos(angles)[:, None], jnp.sin(angles)[:, None])


def upper_flag(my_index, level):
    return my_index // (1 << level) % 2 == 1


def dft_tables(row_count):
    steps_idx = jnp.arange(row_count, dtype=jnp.int32)
    products = steps_idx[:, None] * steps_idx[None, :] % row_count
    angles = TWO_PI * products.astype(jnp.float32) / row_count
    return (jnp.cos(angles), jnp.sin(angles))


def forward_butterfly(signal):
    shard_count = lax.axis_size("seq")
    bit_count = shard_count.bit_length() - 1
    my_index = lax.axis_index("seq")
    row_count = signal.shape[0]
    top_level = bit_count - 1
    partner = swapped(signal, "seq", top_level)
    cos_t, sin_t = twiddle(my_index, top_level, row_count)
    upper_half = upper_flag(my_index, top_level)
    difference = partner - signal
    real_part = jnp.where(upper_half, difference * cos_t, signal + partner)
    imag_part = jnp.where(upper_half, difference * sin_t, jnp.zeros_like(signal))
    for level in range(top_level - 1, -1, -1):
        other_re, other_im = swapped((real_part, imag_part), "seq", level)
        cos_t, sin_t = twiddle(my_index, level, row_count)
        upper_half = upper_flag(my_index, level)
        diff_re = other_re - real_part
        diff_im = other_im - imag_part
        new_re = jnp.where(upper_half, diff_re * cos_t - diff_im * sin_t, real_part + other_re)
        new_im = jnp.where(upper_half, diff_re * sin_t + diff_im * cos_t, imag_part + other_im)
        real_part, imag_part = (new_re, new_im)
    cos_m, sin_m = dft_tables(row_count)
    matrix = jnp.concatenate(
        [jnp.concatenate([cos_m, sin_m], 1), jnp.concatenate([-sin_m, cos_m], 1)], 0
    )
    stacked = jnp.concatenate([real_part, imag_part], 0)
    spectrum = jnp.dot(matrix, stacked, precision=HIGHEST)
    return (spectrum[:row_count], spectrum[row_count:])


def spread_filter(filter_real, filter_imag):
    shard_count = lax.axis_size("seq")
    bit_count = shard_count.bit_length() - 1
    row_count, chan_width = filter_real.shape

    def reorder(table):
        split_bits = table.reshape((row_count // shard_count,) + (2,) * bit_count + (chan_width,))
        order = (0,) + tuple(range(bit_count, 0, -1)) + (bit_count + 1,)
        return jnp.transpose(split_bits, order).reshape(
            row_count // shard_count, shard_count, chan_width
        )

    got_re, got_im = (
        lax.all_to_all(reorder(filter_real), "seq", split_axis=1, concat_axis=0, tiled=True),
        lax.all_to_all(reorder(filter_imag), "seq", split_axis=1, concat_axis=0, tiled=True),
    )
    return (got_re.reshape(row_count, chan_width), got_im.reshape(row_count, chan_width))


def inverse_butterfly(spec_re, spec_im):
    shard_count = lax.axis_size("seq")
    bit_count = shard_count.bit_length() - 1
    my_index = lax.axis_index("seq")
    row_count = spec_re.shape[0]
    cos_m, sin_m = dft_tables(row_count)
    matrix = jnp.concatenate(
        [jnp.concatenate([cos_m, -sin_m], 1), jnp.concatenate([sin_m, cos_m], 1)], 0
    )
    stacked = jnp.dot(matrix, jnp.concatenate([spec_re, spec_im], 0), precision=HIGHEST) / row_count
    real_part = stacked[:row_count]
    imag_part = stacked[row_count:]
    for level in range(bit_count):
        other_re, other_im = swapped((real_part, imag_part), "seq", level)
        cos_t, sin_t = twiddle(my_index, level, row_count)
        upper_half = upper_flag(my_index, level)
        source_re = jnp.where(upper_half, real_part, other_re)
        source_im = jnp.where(upper_half, imag_part, other_im)
        base_re = jnp.where(upper_half, other_re, real_part)
        base_im = jnp.where(upper_half, other_im, imag_part)
        rotated_re = source_re * cos_t + source_im * sin_t
        rotated_im = source_im * cos_t - source_re * sin_t
        factor = jnp.where(upper_half, -0.5, 0.5)
        real_part = 0.5 * base_re + factor * rotated_re
        imag_part = 0.5 * base_im + factor * rotated_im
    return real_part


def shards(features, w_in, filter_real, filter_imag, skip_gain):
    gathered = lax.all_gather(features, "chan", axis=1, tiled=True)
    chan_width = w_in.shape[2]
    row_count = gathered.shape[0]
    add_rows = fold_into(gathered)
    zero_sum = jnp.zeros((row_count, 3 * chan_width), jnp.float32)
    projected = add_rows(zero_sum, lax.all_gather(w_in, "seq", axis=0, tiled=True), jnp.int32(0))
    input_gate = projected[:, :chan_width].astype(jnp.bfloat16)
    value_stream = projected[:, chan_width : 2 * chan_width].astype(jnp.bfloat16)
    output_gate = projected[:, 2 * chan_width :].astype(jnp.bfloat16)
    signal = input_gate.astype(jnp.float32) * value_stream.astype(jnp.float32)
    spec_re, spec_im = forward_butterfly(signal)
    resp_re, resp_im = spread_filter(filter_real, filter_imag)
    prod_re = resp_re * spec_re - resp_im * spec_im
    prod_im = resp_re * spec_im + resp_im * spec_re
    convolved = inverse_butterfly(prod_re, prod_im)
    result = output_gate.astype(jnp.float32) * (convolved + skip_gain[None, :] * signal)
    return result.astype(jnp.bfloat16)


def solution(mesh):
    placed = (
        P("seq", "chan"),
        P("seq", None, "chan"),
        P("seq", "chan"),
        P("seq", "chan"),
        P("chan"),
    )
    return jax.shard_map(
        shards, mesh=mesh, in_specs=placed, out_specs=P("seq", "chan"), check_vma=False
    )
```

profile of v0, /device:TPU:10, one launch (start us, length us, event | category | flops | bytes accessed | tf_op | source)
XLA Modules:
  0.0 793.8 jit_solution(4265865259562781646)
XLA Ops:
  8.0 325.0 %all-gather.5.cloned.1.call-done = bf16[4096,3,512]{2,0,1:T(8,128)(2,1)} async-done(((bf16[64,3,512]{2,0,1:T(8,128)(2,1)}), bf16[4096,3,512]{2,0,1:T(8,128)(2,1)}) %all-gather.5.cloned.1.call-update) | async-done | bytes 12582928 | tf_op jit(solution)/shard_map/all_gather | solution.py:132
  333.0 17.0 %copy.11 = bf16[4096,3,512]{0,2,1:T(8,128)(2,1)} copy(bf16[4096,3,512]{2,0,1:T(8,128)(2,1)} %all-gather.5.cloned.1.call-done) | data formatting | bytes 25165824 | tf_op jit(solution)/shard_map/all_gather | solution.py:132
  350.1 13.4 %all-gather.3.cloned.1.call-done = bf16[256,4096]{1,0:T(8,128)(2,1)} async-done(((bf16[256,1024]{1,0:T(8,128)(2,1)}), bf16[256,4096]{1,0:T(8,128)(2,1)}) %all-gather.3.cloned.1.call-update) | async-done | bytes 2097168 | tf_op jit(solution)/shard_map/all_gather | solution.py:127
  363.5 8.6 %convolution_convert_fusion = bf16[256,1536]{1,0:T(8,128)(2,1)S(1)} fusion(bf16[256,4096]{1,0:T(8,128)(2,1)} %all-gather.3.cloned.1.call-done, bf16[4096,1536]{0,1:T(8,128)(2,1)} %bitcast.17), kind=kOutput, calls=%fused_computation | convolution fusion | flops 3221618688 | bytes 15466496 | tf_op jit(solution)/shard_map/dot_general | solution.py:24
  373.8 12.6 %collective-permute-done = f32[256,512]{1,0:T(8,128)S(1)} collective-permute-done((f32[256,512]{1,0:T(8,128)S(1)}, f32[256,512]{1,0:T(8,128)S(1)}, u32[]{:S(2)}, u32[]{:S(2)}) %collective-permute-start) | collective-permute-done | bytes 524320 | tf_op jit(solution)/shard_map/ppermute | solution.py:18
  392.6 18.5 %collective-permute-done.1 = f32[256,512]{1,0:T(8,128)S(1)} collective-permute-done((f32[256,512]{1,0:T(8,128)S(1)}, f32[256,512]{1,0:T(8,128)S(1)}, u32[]{:S(2)}, u32[]{:S(2)}) %collective-permute-start.1) | collective-permute-done | bytes 524320 | tf_op jit(solution)/shard_map/ppermute | solution.py:18
  411.1 25.9 %collective-permute-done.2 = f32[256,512]{1,0:T(8,128)S(1)} collective-permute-done((f32[256,512]{1,0:T(8,128)S(1)}, f32[256,512]{1,0:T(8,128)S(1)}, u32[]{:S(2)}, u32[]{:S(2)}) %collective-permute-start.2) | collective-permute-done | bytes 524320 | tf_op jit(solution)/shard_map/ppermute | solution.py:18
  442.5 34.0 %collective-permute-done.3 = f32[256,512]{1,0:T(8,128)S(1)} collective-permute-done((f32[256,512]{1,0:T(8,128)S(1)}, f32[256,512]{1,0:T(8,128)S(1)}, u32[]{:S(2)}, u32[]{:S(2)}) %collective-permute-start.3) | collective-permute-done | bytes 524320 | tf_op jit(solution)/shard_map/ppermute | solution.py:18
  476.4 11.2 %collective-permute-done.4 = f32[256,512]{1,0:T(8,128)S(1)} collective-permute-done((f32[256,512]{1,0:T(8,128)S(1)}, f32[256,512]{1,0:T(8,128)S(1)}, u32[]{:S(2)}, u32[]{:S(2)}) %collective-permute-start.4) | collective-permute-done | bytes 524320 | tf_op jit(solution)/shard_map/ppermute | solution.py:18
  494.3 8.3 %all-to-all-start = ((f32[4,64,512]{2,0,1:T(4,128)}), f32[4,64,512]{2,0,1:T(4,128)S(1)}, u32[]{:S(2)}, u32[]{:S(2)}) async-start(f32[4,64,512]{2,0,1:T(4,128)} %bitcast.2), calls=%async_computation | async-start | bytes 1048576 | tf_op jit(solution)/shard_map/all_to_all | solution.py:92
  505.7 13.7 %collective-permute-done.6 = f32[256,512]{1,0:T(8,128)S(1)} collective-permute-done((f32[256,512]{1,0:T(8,128)S(1)}, f32[256,512]{1,0:T(8,128)S(1)}, u32[]{:S(2)}, u32[]{:S(2)}) %collective-permute-start.6) | collective-permute-done | bytes 524320 | tf_op jit(solution)/shard_map/ppermute | solution.py:18
  529.7 7.3 all-to-all-start.1
  538.6 14.2 %collective-permute-done.8 = f32[256,512]{1,0:T(8,128)} collective-permute-done((f32[256,512]{1,0:T(8,128)S(1)}, f32[256,512]{1,0:T(8,128)}, u32[]{:S(2)}, u32[]{:S(2)}) %collective-permute-start.8) | collective-permute-done | bytes 524320 | tf_op jit(solution)/shard_map/ppermute | solution.py:18
  561.0 9.2 %collective-permute-done.10 = f32[256,512]{1,0:T(8,128)S(1)} collective-permute-done((f32[256,512]{1,0:T(8,128)}, f32[256,512]{1,0:T(8,128)S(1)}, u32[]{:S(2)}, u32[]{:S(2)}) %collective-permute-start.10) | collective-permute-done | bytes 524320 | tf_op jit(solution)/shard_map/ppermute | solution.py:18
  570.1 7.3 collective-permute-done.9
  587.5 12.8 %collective-permute-done.11 = f32[256,512]{1,0:T(8,128)S(1)} collective-permute-done((f32[256,512]{1,0:T(8,128)S(1)}, f32[256,512]{1,0:T(8,128)S(1)}, u32[]{:S(2)}, u32[]{:S(2)}) %collective-permute-start.11) | collective-permute-done | bytes 524320 | tf_op jit(solution)/shard_map/ppermute | solution.py:18
  613.2 12.5 %collective-permute-done.13 = f32[256,512]{1,0:T(8,128)S(1)} collective-permute-done((f32[256,512]{1,0:T(8,128)S(1)}, f32[256,512]{1,0:T(8,128)S(1)}, u32[]{:S(2)}, u32[]{:S(2)}) %collective-permute-start.13) | collective-permute-done | bytes 524320 | tf_op jit(solution)/shard_map/ppermute | solution.py:18
  634.9 11.8 %collective-permute-done.15 = f32[256,512]{1,0:T(8,128)S(1)} collective-permute-done((f32[256,512]{1,0:T(8,128)S(1)}, f32[256,512]{1,0:T(8,128)S(1)}, u32[]{:S(2)}, u32[]{:S(2)}) %collective-permute-start.15) | collective-permute-done | bytes 524320 | tf_op jit(solution)/shard_map/ppermute | solution.py:18
  646.7 7.0 collective-permute-done.16
  658.1 26.9 %collective-permute-done.17 = f32[256,512]{1,0:T(8,128)S(1)} collective-permute-done((f32[256,512]{1,0:T(8,128)S(1)}, f32[256,512]{1,0:T(8,128)S(1)}, u32[]{:S(2)}, u32[]{:S(2)}) %collective-permute-start.17) | collective-permute-done | bytes 524320 | tf_op jit(solution)/shard_map/ppermute | solution.py:18
  685.0 56.0 %collective-permute-done.18 = f32[256,512]{1,0:T(8,128)} collective-permute-done((f32[256,512]{1,0:T(8,128)S(1)}, f32[256,512]{1,0:T(8,128)}, u32[]{:S(2)}, u32[]{:S(2)}) %collective-permute-start.18) | collective-permute-done | bytes 524320 | tf_op jit(solution)/shard_map/ppermute | solution.py:18
  748.3 13.6 %collective-permute-done.19 = f32[256,512]{1,0:T(8,128)S(1)} collective-permute-done((f32[256,512]{1,0:T(8,128)S(1)}, f32[256,512]{1,0:T(8,128)S(1)}, u32[]{:S(2)}, u32[]{:S(2)}) %collective-permute-start.19) | collective-permute-done | bytes 524320 | tf_op jit(solution)/shard_map/ppermute | solution.py:18
  762.0 7.7 collective-permute-done.20
  773.2 7.2 collective-permute-done.21
  (77 shorter events, 98.4 us)
Async XLA Ops:
  6.5 326.5 %all-gather.5.cloned.1.call-start = ((), (), s32[]{:S(2)}) async-start(), calls=%async_computation.3 | async-start | bytes 12779520 | tf_op jit(solution)/shard_map/all_gather | solution.py:132
  7.3 356.2 %all-gather.3.cloned.1.call-start = ((), (), s32[]{:S(2)}) async-start(), calls=%async_computation.2 | async-start | bytes 2621440 | tf_op jit(solution)/shard_map/all_gather | solution.py:127
  386.5 24.6 %collective-permute-start.1 = (f32[256,512]{1,0:T(8,128)S(1)}, f32[256,512]{1,0:T(8,128)S(1)}, u32[]{:S(2)}, u32[]{:S(2)}) collective-permute-start(f32[256,512]{1,0:T(8,128)S(1)} %get-tuple-element.27), channel_id=1, source_target_pairs={{0,64},{64,0},{4,68},{68,4},{8,72},{72,8},{12,76},{76,12},{16,80},... | collective-permute-start | bytes 1572872 | tf_op jit(solution)/shard_map/ppermute | solution.py:18
  392.3 44.7 %collective-permute-start.2 = (f32[256,512]{1,0:T(8,128)S(1)}, f32[256,512]{1,0:T(8,128)S(1)}, u32[]{:S(2)}, u32[]{:S(2)}) collective-permute-start(f32[256,512]{1,0:T(8,128)S(1)} %get-tuple-element.28), channel_id=1, source_target_pairs={{0,64},{64,0},{4,68},{68,4},{8,72},{72,8},{12,76},{76,12},{16,80},... | collective-permute-start | bytes 1572872 | tf_op jit(solution)/shard_map/ppermute | solution.py:18
  439.2 37.3 %collective-permute-start.3 = (f32[256,512]{1,0:T(8,128)S(1)}, f32[256,512]{1,0:T(8,128)S(1)}, u32[]{:S(2)}, u32[]{:S(2)}) collective-permute-start(f32[256,512]{1,0:T(8,128)S(1)} %get-tuple-element.23), channel_id=1, source_target_pairs={{0,32},{32,0},{4,36},{36,4},{8,40},{40,8},{12,44},{44,12},{16,48},... | collective-permute-start | bytes 1572872 | tf_op jit(solution)/shard_map/ppermute | solution.py:18
  442.3 45.3 %collective-permute-start.4 = (f32[256,512]{1,0:T(8,128)S(1)}, f32[256,512]{1,0:T(8,128)S(1)}, u32[]{:S(2)}, u32[]{:S(2)}) collective-permute-start(f32[256,512]{1,0:T(8,128)S(1)} %get-tuple-element.24), channel_id=1, source_target_pairs={{0,32},{32,0},{4,36},{36,4},{8,40},{40,8},{12,44},{44,12},{16,48},... | collective-permute-start | bytes 1572872 | tf_op jit(solution)/shard_map/ppermute | solution.py:18
  489.7 16.0 %collective-permute-start.5 = (f32[256,512]{1,0:T(8,128)S(1)}, f32[256,512]{1,0:T(8,128)S(1)}, u32[]{:S(2)}, u32[]{:S(2)}) collective-permute-start(f32[256,512]{1,0:T(8,128)S(1)} %get-tuple-element.21), channel_id=1, source_target_pairs={{0,16},{16,0},{4,20},{20,4},{8,24},{24,8},{12,28},{28,12},{32,48},... | collective-permute-start | bytes 1572872 | tf_op jit(solution)/shard_map/ppermute | solution.py:18
  489.8 29.6 %collective-permute-start.6 = (f32[256,512]{1,0:T(8,128)S(1)}, f32[256,512]{1,0:T(8,128)S(1)}, u32[]{:S(2)}, u32[]{:S(2)}) collective-permute-start(f32[256,512]{1,0:T(8,128)S(1)} %get-tuple-element.22), channel_id=1, source_target_pairs={{0,16},{16,0},{4,20},{20,4},{8,24},{24,8},{12,28},{28,12},{32,48},... | collective-permute-start | bytes 1572872 | tf_op jit(solution)/shard_map/ppermute | solution.py:18
  494.3 35.4 %all-to-all-start = ((f32[4,64,512]{2,0,1:T(4,128)}), f32[4,64,512]{2,0,1:T(4,128)S(1)}, u32[]{:S(2)}, u32[]{:S(2)}) async-start(f32[4,64,512]{2,0,1:T(4,128)} %bitcast.2), calls=%async_computation | async-start | bytes 1048576 | tf_op jit(solution)/shard_map/all_to_all | solution.py:92
  521.7 16.9 %collective-permute-start.7 = (f32[256,512]{1,0:T(8,128)S(1)}, f32[256,512]{1,0:T(8,128)S(1)}, u32[]{:S(2)}, u32[]{:S(2)}) collective-permute-start(f32[256,512]{1,0:T(8,128)S(1)} %get-tuple-element.19), channel_id=1, source_target_pairs={{0,8},{8,0},{4,12},{12,4},{16,24},{24,16},{20,28},{28,20},{32,40},... | collective-permute-start | bytes 1572872 | tf_op jit(solution)/shard_map/ppermute | solution.py:18
  523.9 28.9 %collective-permute-start.8 = (f32[256,512]{1,0:T(8,128)S(1)}, f32[256,512]{1,0:T(8,128)}, u32[]{:S(2)}, u32[]{:S(2)}) collective-permute-start(f32[256,512]{1,0:T(8,128)S(1)} %get-tuple-element.20), channel_id=1, source_target_pairs={{0,8},{8,0},{4,12},{12,4},{16,24},{24,16},{20,28},{28,20},{32,40},... | collective-permute-start | bytes 1572872 | tf_op jit(solution)/shard_map/ppermute | solution.py:18
  529.7 31.1 %all-to-all-start.1 = ((f32[4,64,512]{2,0,1:T(4,128)}), f32[4,64,512]{2,0,1:T(4,128)S(1)}, u32[]{:S(2)}, u32[]{:S(2)}) async-start(f32[4,64,512]{2,0,1:T(4,128)} %bitcast.6), calls=%async_computation.1 | async-start | bytes 1048576 | tf_op jit(solution)/shard_map/all_to_all | solution.py:93
  555.1 15.1 %collective-permute-start.10 = (f32[256,512]{1,0:T(8,128)}, f32[256,512]{1,0:T(8,128)S(1)}, u32[]{:S(2)}, u32[]{:S(2)}) collective-permute-start(f32[256,512]{1,0:T(8,128)} %get-tuple-element.18), channel_id=1, source_target_pairs={{0,4},{4,0},{8,12},{12,8},{16,20},{20,16},{24,28},{28,24},{32,36},... | collective-permute-start | bytes 1572872 | tf_op jit(solution)/shard_map/ppermute | solution.py:18
  556.6 20.9 %collective-permute-start.9 = (f32[256,512]{1,0:T(8,128)S(1)}, f32[256,512]{1,0:T(8,128)}, u32[]{:S(2)}, u32[]{:S(2)}) collective-permute-start(f32[256,512]{1,0:T(8,128)S(1)} %get-tuple-element.17), channel_id=1, source_target_pairs={{0,4},{4,0},{8,12},{12,8},{16,20},{20,16},{24,28},{28,24},{32,36},... | collective-permute-start | bytes 1572872 | tf_op jit(solution)/shard_map/ppermute | solution.py:18
  585.4 14.9 %collective-permute-start.11 = (f32[256,512]{1,0:T(8,128)S(1)}, f32[256,512]{1,0:T(8,128)S(1)}, u32[]{:S(2)}, u32[]{:S(2)}) collective-permute-start(f32[256,512]{1,0:T(8,128)S(1)} %get-tuple-element.29), channel_id=1, source_target_pairs={{0,4},{4,0},{8,12},{12,8},{16,20},{20,16},{24,28},{28,24},{32,36},... | collective-permute-start | bytes 1572872 | tf_op jit(solution)/shard_map/ppermute | solution.py:18
  587.0 19.8 %collective-permute-start.12 = (f32[256,512]{1,0:T(8,128)S(1)}, f32[256,512]{1,0:T(8,128)}, u32[]{:S(2)}, u32[]{:S(2)}) collective-permute-start(f32[256,512]{1,0:T(8,128)S(1)} %get-tuple-element.30), channel_id=1, source_target_pairs={{0,4},{4,0},{8,12},{12,8},{16,20},{20,16},{24,28},{28,24},{32,36},... | collective-permute-start | bytes 1572872 | tf_op jit(solution)/shard_map/ppermute | solution.py:18
  608.1 17.6 %collective-permute-start.13 = (f32[256,512]{1,0:T(8,128)S(1)}, f32[256,512]{1,0:T(8,128)S(1)}, u32[]{:S(2)}, u32[]{:S(2)}) collective-permute-start(f32[256,512]{1,0:T(8,128)S(1)} %get-tuple-element.13), channel_id=1, source_target_pairs={{0,8},{8,0},{4,12},{12,4},{16,24},{24,16},{20,28},{28,20},{32,40},... | collective-permute-start | bytes 1572872 | tf_op jit(solution)/shard_map/ppermute | solution.py:18
  612.9 18.5 %collective-permute-start.14 = (f32[256,512]{1,0:T(8,128)S(1)}, f32[256,512]{1,0:T(8,128)}, u32[]{:S(2)}, u32[]{:S(2)}) collective-permute-start(f32[256,512]{1,0:T(8,128)S(1)} %get-tuple-element.14), channel_id=1, source_target_pairs={{0,8},{8,0},{4,12},{12,4},{16,24},{24,16},{20,28},{28,20},{32,40},... | collective-permute-start | bytes 1572872 | tf_op jit(solution)/shard_map/ppermute | solution.py:18
  633.6 20.1 %collective-permute-start.16 = (f32[256,512]{1,0:T(8,128)S(1)}, f32[256,512]{1,0:T(8,128)}, u32[]{:S(2)}, u32[]{:S(2)}) collective-permute-start(f32[256,512]{1,0:T(8,128)S(1)} %get-tuple-element.12), channel_id=1, source_target_pairs={{0,16},{16,0},{4,20},{20,4},{8,24},{24,8},{12,28},{28,12},{32,48},... | collective-permute-start | bytes 1572872 | tf_op jit(solution)/shard_map/ppermute | solution.py:18
  655.1 29.9 %collective-permute-start.17 = (f32[256,512]{1,0:T(8,128)S(1)}, f32[256,512]{1,0:T(8,128)S(1)}, u32[]{:S(2)}, u32[]{:S(2)}) collective-permute-start(f32[256,512]{1,0:T(8,128)S(1)} %get-tuple-element.9), channel_id=1, source_target_pairs={{0,32},{32,0},{4,36},{36,4},{8,40},{40,8},{12,44},{44,12},{16,48},... | collective-permute-start | bytes 1572872 | tf_op jit(solution)/shard_map/ppermute | solution.py:18
  655.2 85.8 %collective-permute-start.18 = (f32[256,512]{1,0:T(8,128)S(1)}, f32[256,512]{1,0:T(8,128)}, u32[]{:S(2)}, u32[]{:S(2)}) collective-permute-start(f32[256,512]{1,0:T(8,128)S(1)} %get-tuple-element.10), channel_id=1, source_target_pairs={{0,32},{32,0},{4,36},{36,4},{8,40},{40,8},{12,44},{44,12},{16,48},... | collective-permute-start | bytes 1572872 | tf_op jit(solution)/shard_map/ppermute | solution.py:18
  742.3 19.6 %collective-permute-start.19 = (f32[256,512]{1,0:T(8,128)S(1)}, f32[256,512]{1,0:T(8,128)S(1)}, u32[]{:S(2)}, u32[]{:S(2)}) collective-permute-start(f32[256,512]{1,0:T(8,128)S(1)} %get-tuple-element.7), channel_id=1, source_target_pairs={{0,64},{64,0},{4,68},{68,4},{8,72},{72,8},{12,76},{76,12},{16,80},... | collective-permute-start | bytes 1572872 | tf_op jit(solution)/shard_map/ppermute | solution.py:18
  742.4 27.3 %collective-permute-start.20 = (f32[256,512]{1,0:T(8,128)S(1)}, f32[256,512]{1,0:T(8,128)}, u32[]{:S(2)}, u32[]{:S(2)}) collective-permute-start(f32[256,512]{1,0:T(8,128)S(1)} %get-tuple-element.8), channel_id=1, source_target_pairs={{0,64},{64,0},{4,68},{68,4},{8,72},{72,8},{12,76},{76,12},{16,80},... | collective-permute-start | bytes 1572872 | tf_op jit(solution)/shard_map/ppermute | solution.py:18
  771.2 14.8 %collective-permute-start.22 = (f32[256,512]{1,0:T(8,128)S(1)}, f32[256,512]{1,0:T(8,128)S(1)}, u32[]{:S(2)}, u32[]{:S(2)}) collective-permute-start(f32[256,512]{1,0:T(8,128)S(1)} %get-tuple-element.6), channel_id=1, source_target_pairs={{0,128},{128,0},{4,132},{132,4},{8,136},{136,8},{12,140},{140,12},... | collective-permute-start | bytes 1572872 | tf_op jit(solution)/shard_map/ppermute | solution.py:18
  (9 other events, 271.5 us)
Sparse Core Ops, SparseCore 0:
  9.1 323.8 all-gather.4
  334.9 28.5 all-gather.2
where the time goes:
time: 795 us; the launch traced here: 794 us
  waiting for transfers between devices  666 us (84%)
  starting transfers between devices  54.7 us (7%)
  local copies, waits for them, and re-layouts  24.9 us (3%)
  other arithmetic  19.8 us (2%)
  matrix products  14.7 us (2%)
  between operations  13.7 us (2%)
    all_gather x1, waiting for transfers between devices, shards(): lax.all_gather(w_in, 'seq', axis=0, tiled=True)  325 us
    ppermute x23, waiting for transfers between devices, swapped(): return lax.ppermute(block, axis, route)  324 us
    ppermute x23, starting transfers between devices, swapped(): return lax.ppermute(block, axis, route)  39 us
    all_gather x1, local copies, waits for them, and re-layouts, shards(): lax.all_gather(w_in, 'seq', axis=0, tiled=True)  17 us
  transfers between devices with their start and end apart: 27, of which 26 were waited for; matrix products, arithmetic and copies ran while one was open for 4% of the time, Pallas kernels for 0%

commit v1 on v0

--- a/solution.py
+++ b/solution.py
@@ -129,7 +129,13 @@
     row_count = gathered.shape[0]
     add_rows = fold_into(gathered)
     zero_sum = jnp.zeros((row_count, 3 * chan_width), jnp.float32)
-    projected = add_rows(zero_sum, lax.all_gather(w_in, "seq", axis=0, tiled=True), jnp.int32(0))
+    projected = add_rows(
+        zero_sum,
+        jnp.concatenate(
+            lax.all_to_all(jnp.stack([w_in] * lax.axis_size("seq")), "seq", 0, 0), axis=0
+        ),
+        jnp.int32(0),
+    )
     input_gate = projected[:, :chan_width].astype(jnp.bfloat16)
     value_stream = projected[:, chan_width : 2 * chan_width].astype(jnp.bfloat16)
     output_gate = projected[:, 2 * chan_width :].astype(jnp.bfloat16)

time: 795 us -> 752 us (0.946)
  waiting for transfers between devices: 666 us -> 557 us
  starting transfers between devices: 54.7 us -> 96.8 us
  local copies, waits for them, and re-layouts: 24.9 us -> 42.4 us
    all_gather x1 -> x0, waiting for transfers between devices: 325 us -> none  [shards(): lax.all_gather(w_in, 'seq', axis=0, tiled=True)]
    all_to_all x0 -> x1, waiting for transfers between devices: none -> 273 us  [shards(): lax.all_to_all(jnp.stack([w_in] * lax.axis_size('seq')), 'seq', 0, 0)]
    ppermute x23, waiting for transfers between devices: 324 us -> 283 us  [swapped(): return lax.ppermute(block, axis, route)]
    ppermute x23, starting transfers between devices: 39 us -> 62.2 us  [swapped(): return lax.ppermute(block, axis, route)]
    all_gather x1 -> x0, local copies, waits for them, and re-layouts: 17 us -> none  [shards(): lax.all_gather(w_in, 'seq', axis=0, tiled=True)]
    all_to_all x0 -> x1, local copies, waits for them, and re-layouts: none -> 16.7 us  [shards(): lax.all_to_all(jnp.stack([w_in] * lax.axis_size('seq')), 'seq', 0, 0)]
    all_gather x1, waiting for transfers between devices: 13.4 us -> 0.01 us  [shards(): gathered = lax.all_gather(features, 'chan', axis=1, tiled=True)]
    all_to_all x0 -> x1, starting transfers between devices: none -> 13.2 us  [shards(): lax.all_to_all(jnp.stack([w_in] * lax.axis_size('seq')), 'seq', 0, 0)]
  transfers between devices with their start and end apart: 27 -> 27, of which waited for: 26 -> 23; matrix products, arithmetic and copies ran while one was open for 4% -> 5% of each run, Pallas kernels for 0% -> 0%
where the time goes in v1:
time: 752 us; the launch traced here: 745 us
  waiting for transfers between devices  557 us (74%)
  starting transfers between devices  96.8 us (13%)
  local copies, waits for them, and re-layouts  42.4 us (6%)
  other arithmetic  19.8 us (3%)
  matrix products  14.7 us (2%)
  between operations  13.8 us (2%)
    ppermute x23, waiting for transfers between devices, swapped(): return lax.ppermute(block, axis, route)  283 us
    all_to_all x1, waiting for transfers between devices, shards(): lax.all_to_all(jnp.stack([w_in] * lax.axis_size('seq')), 'seq', 0, 0)  273 us
    ppermute x23, starting transfers between devices, swapped(): return lax.ppermute(block, axis, route)  62.2 us
    all_to_all x1, local copies, waits for them, and re-layouts, shards(): lax.all_to_all(jnp.stack([w_in] * lax.axis_size('seq')), 'seq', 0, 0)  16.7 us
  transfers between devices with their start and end apart: 27, of which 23 were waited for; matrix products, arithmetic and copies ran while one was open for 5% of the time, Pallas kernels for 0%

profile of v1, /device:TPU:10, one launch (start us, length us, event | category | flops | bytes accessed | tf_op | source)
XLA Modules:
  0.0 744.6 jit_solution(2113783891510192889)
XLA Ops:
  13.6 13.2 %all-to-all-start = ((bf16[64,64,3,512]{3,1,2,0:T(8,128)(2,1)}), bf16[64,64,3,512]{3,1,2,0:T(8,128)(2,1)}, u32[]{:S(2)}, u32[]{:S(2)}) async-start(bf16[64,64,3,512]{3,1,2,0:T(8,128)(2,1)} %stack.2), calls=%async_computation | async-start | bytes 25165824 | tf_op jit(solution)/shard_map/all_to_all | solution.py:135
  27.5 273.4 %all-to-all-done = bf16[64,64,3,512]{3,1,2,0:T(8,128)(2,1)} async-done(((bf16[64,64,3,512]{3,1,2,0:T(8,128)(2,1)}), bf16[64,64,3,512]{3,1,2,0:T(8,128)(2,1)}, u32[]{:S(2)}, u32[]{:S(2)}) %all-to-all-start) | async-done | bytes 12582944 | tf_op jit(solution)/shard_map/all_to_all | solution.py:135
  300.9 16.7 %copy.12 = bf16[64,64,3,512]{3,2,1,0:T(4,128)(2,1)S(1)} copy(bf16[64,64,3,512]{3,1,2,0:T(8,128)(2,1)} %all-to-all-done) | data formatting | bytes 25165824 | tf_op jit(solution)/shard_map/all_to_all | solution.py:135
  317.7 10.8 %copy.15 = bf16[512,8,3,512]{3,1,2,0:T(8,128)(2,1)} copy(bf16[512,8,3,512]{3,2,1,0:T(4,128)(2,1)S(1)} %bitcast.19) | data formatting | bytes 25165824
  328.5 8.6 %convolution_convert_fusion = bf16[256,1536]{1,0:T(8,128)(2,1)S(1)} fusion(bf16[256,4096]{1,0:T(8,128)(2,1)} %all-gather.2.cloned.1.call-done, bf16[4096,1536]{1,0:T(8,128)(2,1)} %bitcast.20), kind=kOutput, calls=%fused_computation | convolution fusion | flops 3221618688 | bytes 15466496 | tf_op jit(solution)/shard_map/dot_general | solution.py:24
  337.4 9.1 %collective-permute-done = f32[256,512]{1,0:T(8,128)S(1)} collective-permute-done((f32[256,512]{1,0:T(8,128)S(1)}, f32[256,512]{1,0:T(8,128)S(1)}, u32[]{:S(2)}, u32[]{:S(2)}) %collective-permute-start) | collective-permute-done | bytes 524320 | tf_op jit(solution)/shard_map/ppermute | solution.py:18
  346.6 16.8 %collective-permute-start.1 = (f32[256,512]{1,0:T(8,128)S(1)}, f32[256,512]{1,0:T(8,128)S(1)}, u32[]{:S(2)}, u32[]{:S(2)}) collective-permute-start(f32[256,512]{1,0:T(8,128)S(1)} %get-tuple-element.27), channel_id=1, source_target_pairs={{0,64},{64,0},{4,68},{68,4},{8,72},{72,8},{12,76},{76,12},{16,80},... | collective-permute-start | bytes 1572872 | tf_op jit(solution)/shard_map/ppermute | solution.py:18
  363.5 22.4 %collective-permute-done.1 = f32[256,512]{1,0:T(8,128)S(1)} collective-permute-done((f32[256,512]{1,0:T(8,128)S(1)}, f32[256,512]{1,0:T(8,128)S(1)}, u32[]{:S(2)}, u32[]{:S(2)}) %collective-permute-start.1) | collective-permute-done | bytes 524320 | tf_op jit(solution)/shard_map/ppermute | solution.py:18
  386.0 20.4 %collective-permute-done.2 = f32[256,512]{1,0:T(8,128)S(1)} collective-permute-done((f32[256,512]{1,0:T(8,128)S(1)}, f32[256,512]{1,0:T(8,128)S(1)}, u32[]{:S(2)}, u32[]{:S(2)}) %collective-permute-start.2) | collective-permute-done | bytes 524320 | tf_op jit(solution)/shard_map/ppermute | solution.py:18
  411.8 27.9 %collective-permute-done.3 = f32[256,512]{1,0:T(8,128)S(1)} collective-permute-done((f32[256,512]{1,0:T(8,128)S(1)}, f32[256,512]{1,0:T(8,128)S(1)}, u32[]{:S(2)}, u32[]{:S(2)}) %collective-permute-start.3) | collective-permute-done | bytes 524320 | tf_op jit(solution)/shard_map/ppermute | solution.py:18
  439.8 11.1 %collective-permute-done.4 = f32[256,512]{1,0:T(8,128)S(1)} collective-permute-done((f32[256,512]{1,0:T(8,128)S(1)}, f32[256,512]{1,0:T(8,128)S(1)}, u32[]{:S(2)}, u32[]{:S(2)}) %collective-permute-start.4) | collective-permute-done | bytes 524320 | tf_op jit(solution)/shard_map/ppermute | solution.py:18
  457.7 12.6 %all-to-all-start.1 = ((f32[4,64,512]{2,0,1:T(4,128)}), f32[4,64,512]{2,0,1:T(4,128)S(1)}, u32[]{:S(2)}, u32[]{:S(2)}) async-start(f32[4,64,512]{2,0,1:T(4,128)} %bitcast.1), calls=%async_computation.1 | async-start | bytes 1048576 | tf_op jit(solution)/shard_map/all_to_all | solution.py:92
  470.4 11.5 %collective-permute-done.6 = f32[256,512]{1,0:T(8,128)S(1)} collective-permute-done((f32[256,512]{1,0:T(8,128)S(1)}, f32[256,512]{1,0:T(8,128)S(1)}, u32[]{:S(2)}, u32[]{:S(2)}) %collective-permute-start.6) | collective-permute-done | bytes 524320 | tf_op jit(solution)/shard_map/ppermute | solution.py:18
  484.2 8.5 %collective-permute-start.7 = (f32[256,512]{1,0:T(8,128)S(1)}, f32[256,512]{1,0:T(8,128)S(1)}, u32[]{:S(2)}, u32[]{:S(2)}) collective-permute-start(f32[256,512]{1,0:T(8,128)S(1)} %get-tuple-element.19), channel_id=1, source_target_pairs={{0,8},{8,0},{4,12},{12,4},{16,24},{24,16},{20,28},{28,20},{32,40},... | collective-permute-start | bytes 1572872 | tf_op jit(solution)/shard_map/ppermute | solution.py:18
  495.2 8.7 %all-to-all-start.2 = ((f32[4,64,512]{2,0,1:T(4,128)}), f32[4,64,512]{2,0,1:T(4,128)S(1)}, u32[]{:S(2)}, u32[]{:S(2)}) async-start(f32[4,64,512]{2,0,1:T(4,128)} %bitcast.5), calls=%async_computation.2 | async-start | bytes 1048576 | tf_op jit(solution)/shard_map/all_to_all | solution.py:93
  505.9 15.1 %collective-permute-done.8 = f32[256,512]{1,0:T(8,128)} collective-permute-done((f32[256,512]{1,0:T(8,128)S(1)}, f32[256,512]{1,0:T(8,128)}, u32[]{:S(2)}, u32[]{:S(2)}) %collective-permute-start.8) | collective-permute-done | bytes 524320 | tf_op jit(solution)/shard_map/ppermute | solution.py:18
  550.5 9.9 %collective-permute-done.11 = f32[256,512]{1,0:T(8,128)S(1)} collective-permute-done((f32[256,512]{1,0:T(8,128)S(1)}, f32[256,512]{1,0:T(8,128)S(1)}, u32[]{:S(2)}, u32[]{:S(2)}) %collective-permute-start.11) | collective-permute-done | bytes 524320 | tf_op jit(solution)/shard_map/ppermute | solution.py:18
  573.8 11.1 %collective-permute-done.13 = f32[256,512]{1,0:T(8,128)S(1)} collective-permute-done((f32[256,512]{1,0:T(8,128)S(1)}, f32[256,512]{1,0:T(8,128)S(1)}, u32[]{:S(2)}, u32[]{:S(2)}) %collective-permute-start.13) | collective-permute-done | bytes 524320 | tf_op jit(solution)/shard_map/ppermute | solution.py:18
  596.1 11.4 %collective-permute-done.15 = f32[256,512]{1,0:T(8,128)S(1)} collective-permute-done((f32[256,512]{1,0:T(8,128)S(1)}, f32[256,512]{1,0:T(8,128)S(1)}, u32[]{:S(2)}, u32[]{:S(2)}) %collective-permute-start.15) | collective-permute-done | bytes 524320 | tf_op jit(solution)/shard_map/ppermute | solution.py:18
  614.5 10.1 %collective-permute-start.17 = (f32[256,512]{1,0:T(8,128)S(1)}, f32[256,512]{1,0:T(8,128)S(1)}, u32[]{:S(2)}, u32[]{:S(2)}) collective-permute-start(f32[256,512]{1,0:T(8,128)S(1)} %get-tuple-element.9), channel_id=1, source_target_pairs={{0,32},{32,0},{4,36},{36,4},{8,40},{40,8},{12,44},{44,12},{16,48},... | collective-permute-start | bytes 1572872 | tf_op jit(solution)/shard_map/ppermute | solution.py:18
  624.8 28.2 %collective-permute-done.17 = f32[256,512]{1,0:T(8,128)S(1)} collective-permute-done((f32[256,512]{1,0:T(8,128)S(1)}, f32[256,512]{1,0:T(8,128)S(1)}, u32[]{:S(2)}, u32[]{:S(2)}) %collective-permute-start.17) | collective-permute-done | bytes 524320 | tf_op jit(solution)/shard_map/ppermute | solution.py:18
  668.3 31.8 %collective-permute-done.19 = f32[256,512]{1,0:T(8,128)S(1)} collective-permute-done((f32[256,512]{1,0:T(8,128)S(1)}, f32[256,512]{1,0:T(8,128)S(1)}, u32[]{:S(2)}, u32[]{:S(2)}) %collective-permute-start.19) | collective-permute-done | bytes 524320 | tf_op jit(solution)/shard_map/ppermute | solution.py:18
  700.1 12.3 %collective-permute-done.20 = f32[256,512]{1,0:T(8,128)} collective-permute-done((f32[256,512]{1,0:T(8,128)S(1)}, f32[256,512]{1,0:T(8,128)}, u32[]{:S(2)}, u32[]{:S(2)}) %collective-permute-start.20) | collective-permute-done | bytes 524320 | tf_op jit(solution)/shard_map/ppermute | solution.py:18
  715.8 12.8 %collective-permute-done.21 = f32[256,512]{1,0:T(8,128)S(1)} collective-permute-done((f32[256,512]{1,0:T(8,128)S(1)}, f32[256,512]{1,0:T(8,128)S(1)}, u32[]{:S(2)}, u32[]{:S(2)}) %collective-permute-start.21) | collective-permute-done | bytes 524320 | tf_op jit(solution)/shard_map/ppermute | solution.py:18
  (78 shorter events, 116.3 us)
Async XLA Ops:
  13.6 287.3 %all-to-all-start = ((bf16[64,64,3,512]{3,1,2,0:T(8,128)(2,1)}), bf16[64,64,3,512]{3,1,2,0:T(8,128)(2,1)}, u32[]{:S(2)}, u32[]{:S(2)}) async-start(bf16[64,64,3,512]{3,1,2,0:T(8,128)(2,1)} %stack.2), calls=%async_computation | async-start | bytes 25165824 | tf_op jit(solution)/shard_map/all_to_all | solution.py:135
  26.8 301.7 %all-gather.2.cloned.1.call-start = ((), (), s32[]{:S(2)}) async-start(), calls=%async_computation.3 | async-start | bytes 2621440 | tf_op jit(solution)/shard_map/all_gather | solution.py:127
  346.6 39.3 %collective-permute-start.1 = (f32[256,512]{1,0:T(8,128)S(1)}, f32[256,512]{1,0:T(8,128)S(1)}, u32[]{:S(2)}, u32[]{:S(2)}) collective-permute-start(f32[256,512]{1,0:T(8,128)S(1)} %get-tuple-element.27), channel_id=1, source_target_pairs={{0,64},{64,0},{4,68},{68,4},{8,72},{72,8},{12,76},{76,12},{16,80},... | collective-permute-start | bytes 1572872 | tf_op jit(solution)/shard_map/ppermute | solution.py:18
  363.4 43.0 %collective-permute-start.2 = (f32[256,512]{1,0:T(8,128)S(1)}, f32[256,512]{1,0:T(8,128)S(1)}, u32[]{:S(2)}, u32[]{:S(2)}) collective-permute-start(f32[256,512]{1,0:T(8,128)S(1)} %get-tuple-element.28), channel_id=1, source_target_pairs={{0,64},{64,0},{4,68},{68,4},{8,72},{72,8},{12,76},{76,12},{16,80},... | collective-permute-start | bytes 1572872 | tf_op jit(solution)/shard_map/ppermute | solution.py:18
  408.5 31.2 %collective-permute-start.3 = (f32[256,512]{1,0:T(8,128)S(1)}, f32[256,512]{1,0:T(8,128)S(1)}, u32[]{:S(2)}, u32[]{:S(2)}) collective-permute-start(f32[256,512]{1,0:T(8,128)S(1)} %get-tuple-element.23), channel_id=1, source_target_pairs={{0,32},{32,0},{4,36},{36,4},{8,40},{40,8},{12,44},{44,12},{16,48},... | collective-permute-start | bytes 1572872 | tf_op jit(solution)/shard_map/ppermute | solution.py:18
  411.7 39.2 %collective-permute-start.4 = (f32[256,512]{1,0:T(8,128)S(1)}, f32[256,512]{1,0:T(8,128)S(1)}, u32[]{:S(2)}, u32[]{:S(2)}) collective-permute-start(f32[256,512]{1,0:T(8,128)S(1)} %get-tuple-element.24), channel_id=1, source_target_pairs={{0,32},{32,0},{4,36},{36,4},{8,40},{40,8},{12,44},{44,12},{16,48},... | collective-permute-start | bytes 1572872 | tf_op jit(solution)/shard_map/ppermute | solution.py:18
  453.0 17.4 %collective-permute-start.5 = (f32[256,512]{1,0:T(8,128)S(1)}, f32[256,512]{1,0:T(8,128)S(1)}, u32[]{:S(2)}, u32[]{:S(2)}) collective-permute-start(f32[256,512]{1,0:T(8,128)S(1)} %get-tuple-element.21), channel_id=1, source_target_pairs={{0,16},{16,0},{4,20},{20,4},{8,24},{24,8},{12,28},{28,12},{32,48},... | collective-permute-start | bytes 1572872 | tf_op jit(solution)/shard_map/ppermute | solution.py:18
  455.0 27.0 %collective-permute-start.6 = (f32[256,512]{1,0:T(8,128)S(1)}, f32[256,512]{1,0:T(8,128)S(1)}, u32[]{:S(2)}, u32[]{:S(2)}) collective-permute-start(f32[256,512]{1,0:T(8,128)S(1)} %get-tuple-element.22), channel_id=1, source_target_pairs={{0,16},{16,0},{4,20},{20,4},{8,24},{24,8},{12,28},{28,12},{32,48},... | collective-permute-start | bytes 1572872 | tf_op jit(solution)/shard_map/ppermute | solution.py:18
  457.7 37.5 %all-to-all-start.1 = ((f32[4,64,512]{2,0,1:T(4,128)}), f32[4,64,512]{2,0,1:T(4,128)S(1)}, u32[]{:S(2)}, u32[]{:S(2)}) async-start(f32[4,64,512]{2,0,1:T(4,128)} %bitcast.1), calls=%async_computation.1 | async-start | bytes 1048576 | tf_op jit(solution)/shard_map/all_to_all | solution.py:92
  484.2 21.7 %collective-permute-start.7 = (f32[256,512]{1,0:T(8,128)S(1)}, f32[256,512]{1,0:T(8,128)S(1)}, u32[]{:S(2)}, u32[]{:S(2)}) collective-permute-start(f32[256,512]{1,0:T(8,128)S(1)} %get-tuple-element.19), channel_id=1, source_target_pairs={{0,8},{8,0},{4,12},{12,4},{16,24},{24,16},{20,28},{28,20},{32,40},... | collective-permute-start | bytes 1572872 | tf_op jit(solution)/shard_map/ppermute | solution.py:18
  492.6 28.3 %collective-permute-start.8 = (f32[256,512]{1,0:T(8,128)S(1)}, f32[256,512]{1,0:T(8,128)}, u32[]{:S(2)}, u32[]{:S(2)}) collective-permute-start(f32[256,512]{1,0:T(8,128)S(1)} %get-tuple-element.20), channel_id=1, source_target_pairs={{0,8},{8,0},{4,12},{12,4},{16,24},{24,16},{20,28},{28,20},{32,40},... | collective-permute-start | bytes 1572872 | tf_op jit(solution)/shard_map/ppermute | solution.py:18
  495.2 33.7 %all-to-all-start.2 = ((f32[4,64,512]{2,0,1:T(4,128)}), f32[4,64,512]{2,0,1:T(4,128)S(1)}, u32[]{:S(2)}, u32[]{:S(2)}) async-start(f32[4,64,512]{2,0,1:T(4,128)} %bitcast.5), calls=%async_computation.2 | async-start | bytes 1048576 | tf_op jit(solution)/shard_map/all_to_all | solution.py:93
  523.2 17.3 %collective-permute-start.9 = (f32[256,512]{1,0:T(8,128)S(1)}, f32[256,512]{1,0:T(8,128)}, u32[]{:S(2)}, u32[]{:S(2)}) collective-permute-start(f32[256,512]{1,0:T(8,128)S(1)} %get-tuple-element.17), channel_id=1, source_target_pairs={{0,4},{4,0},{8,12},{12,8},{16,20},{20,16},{24,28},{28,24},{32,36},... | collective-permute-start | bytes 1572872 | tf_op jit(solution)/shard_map/ppermute | solution.py:18
  550.2 17.8 %collective-permute-start.12 = (f32[256,512]{1,0:T(8,128)S(1)}, f32[256,512]{1,0:T(8,128)}, u32[]{:S(2)}, u32[]{:S(2)}) collective-permute-start(f32[256,512]{1,0:T(8,128)S(1)} %get-tuple-element.30), channel_id=1, source_target_pairs={{0,4},{4,0},{8,12},{12,8},{16,20},{20,16},{24,28},{28,24},{32,36},... | collective-permute-start | bytes 1572872 | tf_op jit(solution)/shard_map/ppermute | solution.py:18
  569.3 15.6 %collective-permute-start.13 = (f32[256,512]{1,0:T(8,128)S(1)}, f32[256,512]{1,0:T(8,128)S(1)}, u32[]{:S(2)}, u32[]{:S(2)}) collective-permute-start(f32[256,512]{1,0:T(8,128)S(1)} %get-tuple-element.13), channel_id=1, source_target_pairs={{0,8},{8,0},{4,12},{12,4},{16,24},{24,16},{20,28},{28,20},{32,40},... | collective-permute-start | bytes 1572872 | tf_op jit(solution)/shard_map/ppermute | solution.py:18
  573.7 16.9 %collective-permute-start.14 = (f32[256,512]{1,0:T(8,128)S(1)}, f32[256,512]{1,0:T(8,128)}, u32[]{:S(2)}, u32[]{:S(2)}) collective-permute-start(f32[256,512]{1,0:T(8,128)S(1)} %get-tuple-element.14), channel_id=1, source_target_pairs={{0,8},{8,0},{4,12},{12,4},{16,24},{24,16},{20,28},{28,20},{32,40},... | collective-permute-start | bytes 1572872 | tf_op jit(solution)/shard_map/ppermute | solution.py:18
  592.0 15.5 %collective-permute-start.15 = (f32[256,512]{1,0:T(8,128)S(1)}, f32[256,512]{1,0:T(8,128)S(1)}, u32[]{:S(2)}, u32[]{:S(2)}) collective-permute-start(f32[256,512]{1,0:T(8,128)S(1)} %get-tuple-element.11), channel_id=1, source_target_pairs={{0,16},{16,0},{4,20},{20,4},{8,24},{24,8},{12,28},{28,12},{32,48},... | collective-permute-start | bytes 1572872 | tf_op jit(solution)/shard_map/ppermute | solution.py:18
  596.0 17.2 %collective-permute-start.16 = (f32[256,512]{1,0:T(8,128)S(1)}, f32[256,512]{1,0:T(8,128)}, u32[]{:S(2)}, u32[]{:S(2)}) collective-permute-start(f32[256,512]{1,0:T(8,128)S(1)} %get-tuple-element.12), channel_id=1, source_target_pairs={{0,16},{16,0},{4,20},{20,4},{8,24},{24,8},{12,28},{28,12},{32,48},... | collective-permute-start | bytes 1572872 | tf_op jit(solution)/shard_map/ppermute | solution.py:18
  614.5 38.5 %collective-permute-start.17 = (f32[256,512]{1,0:T(8,128)S(1)}, f32[256,512]{1,0:T(8,128)S(1)}, u32[]{:S(2)}, u32[]{:S(2)}) collective-permute-start(f32[256,512]{1,0:T(8,128)S(1)} %get-tuple-element.9), channel_id=1, source_target_pairs={{0,32},{32,0},{4,36},{36,4},{8,40},{40,8},{12,44},{44,12},{16,48},... | collective-permute-start | bytes 1572872 | tf_op jit(solution)/shard_map/ppermute | solution.py:18
  624.7 36.0 %collective-permute-start.18 = (f32[256,512]{1,0:T(8,128)S(1)}, f32[256,512]{1,0:T(8,128)}, u32[]{:S(2)}, u32[]{:S(2)}) collective-permute-start(f32[256,512]{1,0:T(8,128)S(1)} %get-tuple-element.10), channel_id=1, source_target_pairs={{0,32},{32,0},{4,36},{36,4},{8,40},{40,8},{12,44},{44,12},{16,48},... | collective-permute-start | bytes 1572872 | tf_op jit(solution)/shard_map/ppermute | solution.py:18
  662.0 38.0 %collective-permute-start.19 = (f32[256,512]{1,0:T(8,128)S(1)}, f32[256,512]{1,0:T(8,128)S(1)}, u32[]{:S(2)}, u32[]{:S(2)}) collective-permute-start(f32[256,512]{1,0:T(8,128)S(1)} %get-tuple-element.7), channel_id=1, source_target_pairs={{0,64},{64,0},{4,68},{68,4},{8,72},{72,8},{12,76},{76,12},{16,80},... | collective-permute-start | bytes 1572872 | tf_op jit(solution)/shard_map/ppermute | solution.py:18
  667.1 45.2 %collective-permute-start.20 = (f32[256,512]{1,0:T(8,128)S(1)}, f32[256,512]{1,0:T(8,128)}, u32[]{:S(2)}, u32[]{:S(2)}) collective-permute-start(f32[256,512]{1,0:T(8,128)S(1)} %get-tuple-element.8), channel_id=1, source_target_pairs={{0,64},{64,0},{4,68},{68,4},{8,72},{72,8},{12,76},{76,12},{16,80},... | collective-permute-start | bytes 1572872 | tf_op jit(solution)/shard_map/ppermute | solution.py:18
  713.7 14.9 %collective-permute-start.21 = (f32[256,512]{1,0:T(8,128)S(1)}, f32[256,512]{1,0:T(8,128)S(1)}, u32[]{:S(2)}, u32[]{:S(2)}) collective-permute-start(f32[256,512]{1,0:T(8,128)S(1)} %get-tuple-element.5), channel_id=1, source_target_pairs={{0,128},{128,0},{4,132},{132,4},{8,136},{136,8},{12,140},{140,12},... | collective-permute-start | bytes 1572872 | tf_op jit(solution)/shard_map/ppermute | solution.py:18
  715.7 21.1 %collective-permute-start.22 = (f32[256,512]{1,0:T(8,128)S(1)}, f32[256,512]{1,0:T(8,128)S(1)}, u32[]{:S(2)}, u32[]{:S(2)}) collective-permute-start(f32[256,512]{1,0:T(8,128)S(1)} %get-tuple-element.6), channel_id=1, source_target_pairs={{0,128},{128,0},{4,132},{132,4},{8,136},{136,8},{12,140},{140,12},... | collective-permute-start | bytes 1572872 | tf_op jit(solution)/shard_map/ppermute | solution.py:18
  (9 other events, 253.5 us)
Sparse Core Ops, SparseCore 0:
  29.4 47.0 all-gather.1
